TPU v7x, 256 devices: a whole 4x4x8 slice. The times are simulated.
256 devices in a mesh: grp: 8 (over z_hi, x), shard: 32 (over y, z_lo, core).
Axes of the slice: x: 4, y: 4, z: 8 (z_hi: 2, z_lo: 4; z = z_hi * 4 + z_lo), core: 2. Of those that a mesh axis runs over, the one named last changes fastest.
Arguments:
- tokens: bfloat16 [131072, 8192], P(('grp', 'shard')), may hold values from -24 to 24
- norm_gain: float32 [8192], replicated, may hold values from 0.1 to 1.9
- codes: int32 [8192, 512], P('shard'), may hold values from 0 to 15
- zero_points: int32 [64, 512], P('shard'), may hold values from 0 to 15
- scales: float32 [64, 512], P('shard'), may hold values from 0.0008 to 0.008
- key_grad: bfloat16 [131072, 512], P(('grp', 'shard')), may hold values from -0.016479492 to 0.016479492
Outputs:
- keys: bfloat16 [131072, 512], P(('grp', 'shard'))
- weight_grad: float32 [8192, 512], P('shard')
All inputs are finite; a program needn't handle non-finite values.
Results may differ from a plain program's by a relative error of at most 0.0058.
Values may be sent and summed in bfloat16 or wider, within the bound.
A program may use at most 128 MiB of HBM per device.

v0:
```python
import jax
import jax.numpy as jnp
from jax import lax
from jax.sharding import PartitionSpec as P

GROUP = 128


EPS = 1e-05


def normalize(tokens, norm_gain):
    values = tokens.astype(jnp.float32)
    mean_sq = jnp.mean(values * values, axis=-1, keepdims=True)
    return (values * lax.rsqrt(mean_sq + EPS) * norm_gain).astype(jnp.bfloat16)


def dequantize(codes, zero_points, scales):
    groups = scales.shape[0]
    width = codes.shape[1]
    shaped = codes.reshape(groups, GROUP, width) - zero_points[:, None, :]
    weight = shaped.astype(jnp.float32) * scales[:, None, :]
    return weight.astype(jnp.bfloat16).reshape(groups * GROUP, width)


def per_device(tokens, norm_gain, codes, zero_points, scales, key_grad):
    normed = normalize(tokens, norm_gain)
    weight = dequantize(codes, zero_points, scales)
    columns = normed
    keys = jnp.dot(
        columns,
        lax.all_gather(weight, "shard", axis=0, tiled=True),
        preferred_element_type=jnp.float32,
    ).astype(jnp.bfloat16)
    columns = normed
    own_rows = lax.psum_scatter(
        lax.dot_general(
            columns, key_grad, (((0,), (0,)), ((), ())), preferred_element_type=jnp.float32
        ),
        "shard",
        scatter_dimension=0,
        tiled=True,
    )
    weight_grad = lax.psum(own_rows, "grp")
    return (keys, weight_grad)


def solution(mesh):
    in_specs = (
        P(("grp", "shard"), None),
        P(),
        P("shard", None),
        P("shard", None),
        P("shard", None),
        P(("grp", "shard"), None),
    )
    out_specs = (P(("grp", "shard"), None), P("shard", None))
    return jax.shard_map(
        per_device, mesh=mesh, in_specs=in_specs, out_specs=out_specs, check_vma=False
    )
```

profile of v0, /device:TPU:2, one launch (start us, length us, event | category | flops | bytes accessed | tf_op | source)
XLA Modules:
  0.0 403.2 jit_solution(18058780840152596836)
XLA Ops:
  7.2 0.0 copy-start
  7.2 0.0 reduce-scatter.2.cloned.1.call-start
  7.2 5.2 %fusion = f32[512]{0:T(512)S(1)} fusion(bf16[512,8192]{1,0:T(8,128)(2,1)} %param.6), kind=kLoop, calls=%fused_computation.2 | loop fusion | flops 12582400 | bytes 8390656 | tf_op jit(solution)/shard_map/reduce_sum | solution.py:14
  12.4 0.0 copy-done
  12.4 13.3 %fusion.3 = f32[8192,512]{1,0:T(8,128)} fusion(bf16[512,512]{1,0:T(8,128)(2,1)S(1)} %copy-done, bf16[512,8192]{1,0:T(8,128)(2,1)} %param.6, f32[8192]{0:T(1024)} %param.7, f32[512]{0:T(512)S(1)} %add_rsqrt_fusion), kind=kOutput, calls=%fused_computation.5 | convolution fusion | flops 4311744512 | bytes 25724928 | tf_op jit(solution)/shard_map/dot_general | solution.py:37
  25.7 0.0 copy-start.1
  25.7 0.0 copy-start.2
  25.7 0.0 copy-start.3
  25.7 0.0 copy-start.4
  25.7 0.0 reduce-scatter.2.cloned.1.call-update
  25.7 0.0 all-gather.2.cloned.1.call-start
  25.8 1.0 copy-done.1
  26.8 0.0 copy-done.2
  26.8 0.0 copy-done.3
  26.8 0.8 fusion.10
  27.5 0.0 all-gather.2.cloned.1.call-update
  27.6 0.0 all-reduce.2.cloned.1.call-start
  27.6 193.5 %reduce-scatter.2.cloned.1.call-done = f32[256,512]{1,0:T(8,128)} async-done(((f32[8192,512]{1,0:T(8,128)}), f32[256,512]{1,0:T(8,128)}) %reduce-scatter.2.cloned.1.call-update) | async-done | bytes 524304 | tf_op jit(solution)/shard_map/reduce_scatter | solution.py:36
  221.1 0.0 all-reduce.2.cloned.1.call-update
  221.2 69.3 %all-gather.2.cloned.1.call-done = bf16[8192,512]{1,0:T(8,128)(2,1)} async-done(((bf16[256,512]{1,0:T(8,128)(2,1)}), bf16[8192,512]{1,0:T(8,128)(2,1)}) %all-gather.2.cloned.1.call-update) | async-done | bytes 8388624 | tf_op jit(solution)/shard_map/all_gather | solution.py:32
  290.4 0.0 copy-done.4
  290.4 11.1 %fusion.7 = bf16[512,512]{1,0:T(8,128)(2,1)} fusion(bf16[8192,512]{1,0:T(8,128)(2,1)} %all-gather.2.cloned.1.call-done, bf16[512,8192]{1,0:T(8,128)(2,1)} %param.6, f32[8192]{0:T(1024)S(1)} %copy-done.4, f32[512]{0:T(512)S(1)} %add_rsqrt_fusion), kind=kOutput, calls=%fused_computation.7 | convolution fusion | flops 4312006656 | bytes 17336320 | tf_op jit(solution)/shard_map/dot_general | solution.py:30
  301.5 93.3 %all-reduce.2.cloned.1.call-done = f32[256,512]{1,0:T(8,128)} async-done(((f32[256,512]{1,0:T(8,128)}), f32[256,512]{1,0:T(8,128)}) %all-reduce.2.cloned.1.call-update) | async-done | bytes 524304 | tf_op jit(solution)/shard_map/psum | solution.py:44
  394.8 1.9 copy.9
  (1 shorter events, 0.0 us)
Async XLA Ops:
  7.2 5.2 %copy-start = (bf16[512,512]{1,0:T(8,128)(2,1)S(1)}, bf16[512,512]{1,0:T(8,128)(2,1)}, u32[]{:S(2)}) copy-start(bf16[512,512]{1,0:T(8,128)(2,1)} %param.11) | copy-start | bytes 1572868
  7.2 214.0 %reduce-scatter.2.cloned.1.call-start = ((), (), s32[]{:S(2)}) async-start(), calls=%async_computation.2 | async-start | bytes 17301504 | tf_op jit(solution)/shard_map/reduce_scatter | solution.py:36
  25.7 1.0 copy-start.1
  25.7 1.0 copy-start.2
  25.7 1.0 copy-start.3
  25.7 264.7 %copy-start.4 = (f32[8192]{0:T(1024)S(1)}, f32[8192]{0:T(1024)}, u32[]{:S(2)}) copy-start(f32[8192]{0:T(1024)} %param.7) | copy-start | bytes 98308
  25.7 264.7 %all-gather.2.cloned.1.call-start = ((), (), s32[]{:S(2)}) async-start(), calls=%async_computation.1 | async-start | bytes 8650752 | tf_op jit(solution)/shard_map/all_gather | solution.py:32
  27.6 367.3 %all-reduce.2.cloned.1.call-start = ((), (), s32[]{:S(2)}) async-start(), calls=%async_computation.3 | async-start | bytes 1048576 | tf_op jit(solution)/shard_map/psum | solution.py:44
Sparse Core Ops, SparseCore 0:
  25.9 195.2 reduce-scatter.1
  223.6 66.8 all-gather.1
  293.1 101.7 all-reduce.1
where the time goes:
time: 409 us; the launch traced here: 403 us
  waiting for transfers between devices  356 us (87%)
  matrix products  24.4 us (6%)
  between operations  13.8 us (3%)
  other arithmetic  5.93 us (1%)
    reduce_scatter x1, waiting for transfers between devices, per_device(): lax.psum_scatter(lax.dot_general(columns, key_grad, (((0,), (0,)), ((), (...  194 us
    psum x1, waiting for transfers between devices, per_device(): weight_grad = lax.psum(own_rows, 'grp')  93.3 us
    all_gather x1, waiting for transfers between devices, per_device(): lax.all_gather(weight, 'shard', axis=0, tiled=True)  69.3 us
    dot_general x1, matrix products, per_device(): lax.dot_general(columns, key_grad, (((0,), (0,)), ((), ())), preferred_el...  13.3 us
    dot_general x1, matrix products, per_device(): jnp.dot(columns, lax.all_gather(weight, 'shard', axis=0, tiled=True), pre...  11.1 us
  transfers between devices with their start and end apart: 3, of which 3 were waited for; matrix products, arithmetic and copies ran while one was open for 3% of the time, Pallas kernels for 0%

commit v1 on v0

v1 whole, which is shorter than its diff:
```python
import jax
import jax.numpy as jnp
from jax import lax
from jax.experimental import pallas as pl
from jax.experimental.pallas import tpu as pltpu
from jax.sharding import PartitionSpec as P

EPS = 1e-05
D, KV, TOK = 8192, 512, 512
BLK = 256
MESH = pl.DeviceIdType.MESH
BF, F32 = jnp.bfloat16, jnp.float32
ORDER = (0, 1, 3, 2)
BLOCKS = [(0, 0), (0, 1), (0, 3), (1, 0), (3, 0), (0, 2), (2, 0), (1, 1), (1, 3), (3, 1), (3, 3), (1, 2), (3, 2), (2, 1), (2, 3), (2, 2)]
NCH = 16
LAG2, LAGF = 2, 4
SLOT_A, SLOT_B, SLOT_C, SLOT_D = 1, 3, 8, 10
KEYS0 = 3
NT = 8


def gray(i):
    return i + (i // 2) * (1 - 2 * (i % 2))


def pick(table, m):
    value = table[0]
    for n in range(1, len(table)):
        value = jnp.where(m == n, table[n], value)
    return value


def kernel(tok_h, gain_h, codes_h, zp_h, sc_h, kg_h, keys_ref, grad_ref,
           t, w, gain, codes, zp, sc, kg, kt, rkt, rcol, own, psend, prec, comb, xt, xs, xf, ys, ysum, yr, zs, zr, fin, acc,
           lsem, s_p, r_p, s_xt, r_xt, s_xf, r_xf, s_y, r_y, s_z, r_z, s_f, r_f, s_ag, r_ag, s_w, r_w):
    g, s = lax.axis_index("grp"), lax.axis_index("shard")
    x, zh = lax.rem(g, 4), lax.div(g, 4)
    y, zl, c = lax.div(s, 8), lax.rem(lax.div(s, 2), 4), lax.rem(s, 2)
    z = zh * 4 + zl

    def at(ax, ay, az, ac):
        ax, ay, az = lax.rem(ax, 4), lax.rem(ay, 4), lax.rem(az, 8)
        return (lax.div(az, 4) * 4 + ax, (ay * 4 + lax.rem(az, 4)) * 2 + ac)

    partner = at(x, y, z, 1 - c)
    xl, xr = at(x + 3, y, z, c), at(x + 1, y, z, c)
    hop = {("y", 0): at(x, y + 1, z, c), ("y", 1): at(x, y + 3, z, c), ("z", 0): at(x, y, z + 1, c), ("z", 1): at(x, y, z + 7, c)}

    def block(dy, dz, core):
        return (lax.rem(y + dy, 4) * 4 + lax.rem(zl + dz, 4)) * 2 + core

    def send(src, dst, ss, rs, to):
        return pltpu.make_async_remote_copy(src_ref=src, dst_ref=dst, send_sem=ss, recv_sem=rs, device_id=to, device_id_type=MESH)

    loads = [pltpu.make_async_copy(a, b, lsem.at[i]) for i, (a, b) in enumerate(
        [(codes_h, codes), (zp_h, zp), (sc_h, sc), (gain_h, gain), (kg_h, kg)])]
    for cp in loads:
        cp.start()
    rows_t = TOK // NT

    def load_t(i):
        r = pl.ds(pl.multiple_of(i * rows_t, rows_t), rows_t)
        return pltpu.make_async_copy(tok_h.at[r], t.at[r], lsem.at[5 + i])

    for i in range(NT):
        load_t(i).start()

    barrier = pltpu.get_barrier_semaphore()
    peers = [partner] + [at(x + i, y, z, c) for i in (1, 2, 3)] + [at(x, y + i, z, c) for i in (1, 2, 3)]
    peers += [at(x, y, z + i, c) for i in range(1, 8)]
    for p in peers:
        pl.semaphore_signal(barrier, inc=1, device_id=p, device_id_type=MESH)

    for cp in loads[:4]:
        cp.wait()
    mine = block(0, 0, c)
    for j in range(2):
        row = gain[pl.ds(2 * s + j, 1), :]
        col = jnp.transpose(jnp.broadcast_to(row, (128, 128)))
        part = pl.ds(j * 128, 128)
        for q in range(4):
            lanes = pl.ds(q * 128, 128)
            shaped = (codes[part, lanes] - zp[pl.ds(j, 1), lanes]).astype(F32)
            w[mine, part, lanes] = (shaped * sc[pl.ds(j, 1), lanes] * col).astype(BF)

    pl.semaphore_wait(barrier, len(peers))

    def ag(h, n, way, kind):
        axis = ("y", "z")[(h + (n > 0)) % 2]
        dp = ORDER[n - 1] if n > 0 else 0
        off = 0 if kind == 0 else (3, 1)[way]
        if n == 0:
            dp, dq = off, 0
        else:
            dq = off
        dy, dz = (dp, dq) if h == 0 else (dq, dp)
        lo, size = (h * 128, 128) if kind == 0 else (h * 128 + 64 * way, 64)
        ref = w.at[block(dy, dz, c), pl.ds(lo, size)]
        i = ((h * 5 + n) * 2 + way) * 2 + kind
        return send(ref, ref, s_ag.at[i], r_ag.at[i], hop[(axis, way)])

    def ag_start(n, kind):
        for h in range(2):
            for way in range(2):
                ag(h, n, way, kind).start()

    def ag_wait(n, kind):
        for h in range(2):
            for way in range(2):
                ag(h, n, way, kind).wait_recv()

    def share(m):
        dy, dz = BLOCKS[m]
        ref = w.at[block(dy, dz, c)]
        return send(ref, ref, s_w.at[m], r_w.at[m], partner)

    ag_start(0, 0)
    ag_start(1, 0)
    share(0).start()

    loads[4].wait()
    kt[...] = jnp.transpose(kg[...].astype(F32))

    def norm_rows(i, carry):
        load_t(i).wait()

        def tile(u, carry):
            r0 = pl.multiple_of(i * rows_t + u * 16, 16)
            sums = [jnp.zeros((16, 128), F32) for _ in range(4)]
            for v in range(D // 128):
                val = t[pl.ds(r0, 16), pl.ds(v * 128, 128)].astype(F32)
                sums[v % 4] = sums[v % 4] + val * val
            total = jnp.sum((sums[0] + sums[1]) + (sums[2] + sums[3]), axis=1, keepdims=True)
            rcol[pl.ds(r0, 16), :] = jnp.broadcast_to(lax.rsqrt(total * (1.0 / D) + EPS), (16, 128))
            return carry

        return lax.fori_loop(0, rows_t // 16, tile, carry)

    lax.fori_loop(0, NT, norm_rows, 0)
    for q in range(4):
        lanes = pl.ds(q * 128, 128)
        row = jnp.transpose(rcol[lanes, :])[0:1, :]
        rkt[:, lanes] = (kt[:, lanes] * row).astype(BF)

    def place(k):
        return gray(3 - k % 4), gray(k // 4)

    def term(b):
        cols = pl.ds(pl.multiple_of(b * BLK, BLK), BLK)
        return jnp.dot(rkt[...], t[:, cols], preferred_element_type=F32)

    def to_partner(k):
        return send(psend.at[k], prec.at[k], s_p.at[k], r_p.at[k], partner)

    def piece(dx, half):
        return pl.ds(pl.multiple_of(lax.rem(x + dx, 4) * 128 + half * 64, 64), 64)

    def x_first(k):
        return [
            send(comb.at[k, piece(2, 0)], xt.at[0, k], s_xt.at[0, k], r_xt.at[0, k], xl),
            send(comb.at[k, piece(2, 1)], xt.at[1, k], s_xt.at[1, k], r_xt.at[1, k], xr),
            send(comb.at[k, piece(1, 0)], xf.at[0, k], s_xf.at[0, k], r_xf.at[0, k], xr),
            send(comb.at[k, piece(3, 1)], xf.at[1, k], s_xf.at[1, k], r_xf.at[1, k], xl),
        ]

    def x_second(k):
        return [
            send(xs.at[0, k], xf.at[2, k], s_xf.at[2, k], r_xf.at[2, k], xl),
            send(xs.at[1, k], xf.at[3, k], s_xf.at[3, k], r_xf.at[3, k], xr),
        ]

    def to_y(k):
        dy, _ = place(k)
        n = (k // 4) * 3 + k % 4
        return send(ys.at[k], yr.at[n], s_y.at[n], r_y.at[n], at(x, y + dy, z, c))

    def to_z(j, way):
        to = at(x, y, z + gray(j) + 4 * way, c)
        return send(zs.at[j], zr.at[z], s_z.at[j, way], r_z.at[z], to)

    def gradient(k):
        dy, dz = place(k)
        psend[k] = term(block(dy, dz, 1 - c)).astype(BF)
        to_partner(k).start()
        own[k % 2] = term(block(dy, dz, c))

    def combine(k):
        to_partner(k).wait_recv()
        comb[k] = (own[k % 2] + prec[k].astype(F32)).astype(BF)
        for cp in x_first(k):
            cp.start()

    def second(k):
        first = x_first(k)
        later = x_second(k)
        for i, dx in ((0, 3), (1, 1)):
            first[i].wait_recv()
            xs[i, k] = (comb[k, piece(dx, i), :].astype(F32) + xt[i, k].astype(F32)).astype(BF)
            later[i].start()

    def final(k):
        first = x_first(k)
        later = x_second(k)
        for cp in (first[2], first[3], later[0], later[1]):
            cp.wait_recv()
        a = comb[k, piece(0, 0), :].astype(F32) + xf[0, k].astype(F32) + xf[2, k].astype(F32)
        b = comb[k, piece(0, 1), :].astype(F32) + xf[1, k].astype(F32) + xf[3, k].astype(F32)

        @pl.when(k % 4 != 3)
        def _():
            ys[k, pl.ds(0, 64), :] = a.astype(BF)
            ys[k, pl.ds(64, 64), :] = b.astype(BF)
            to_y(k).start()

        @pl.when(k % 4 == 3)
        def _():
            ysum[pl.ds(0, 64), :] = a
            ysum[pl.ds(64, 64), :] = b
            j = k // 4
            for i in range(3):
                to_y(j * 4 + i).wait_recv()
            total = ysum[...]
            for i in range(3):
                total = total + yr[j * 3 + i].astype(F32)
            zs[j] = total.astype(BF)

            @pl.when(j == 0)
            def _():
                zr[z] = total.astype(BF)

            @pl.when(j != 0)
            def _():
                to_z(j, 0).start()

            to_z(j, 1).start()

    def sent(k):
        for cp in [to_partner(k)] + x_first(k) + x_second(k):
            cp.wait_send()

        @pl.when(k % 4 != 3)
        def _():
            to_y(k).wait_send()

    def keys_step(m):
        dy, dz = pick([b[0] for b in BLOCKS], m), pick([b[1] for b in BLOCKS], m)
        ref = w.at[block(dy, dz, 1 - c)]
        send(ref, ref, s_w.at[m], r_w.at[m], partner).wait_recv()
        for core in range(2):
            b = block(dy, dz, core)
            cols = pl.ds(pl.multiple_of(b * BLK, BLK), BLK)
            acc[...] += jnp.dot(t[:, cols], w[b], preferred_element_type=F32)

    acc[...] = jnp.zeros_like(acc)

    def step(k, carry):
        @pl.when(k < NCH)
        def _():
            gradient(k)

        @pl.when(jnp.logical_and(k >= 1, k < NCH + 1))
        def _():
            combine(k - 1)

        @pl.when(k == SLOT_A)
        def _():
            ag_wait(0, 0)
            ag_start(0, 1)
            ag_start(2, 0)
            ag_start(3, 0)
            ag_wait(1, 0)
            ag_start(1, 1)
            for m in range(1, 5):
                share(m).start()

        @pl.when(k == SLOT_B)
        def _():
            ag_wait(0, 1)
            ag_start(4, 0)
            for n in (2, 3):
                ag_wait(n, 0)
                ag_start(n, 1)
            ag_wait(1, 1)
            for m in range(5, 11):
                share(m).start()

        @pl.when(k == SLOT_C)
        def _():
            ag_wait(4, 0)
            ag_start(4, 1)
            ag_wait(2, 1)
            ag_wait(3, 1)
            for m in range(11, 15):
                share(m).start()

        @pl.when(k == SLOT_D)
        def _():
            ag_wait(4, 1)
            share(15).start()

        @pl.when(jnp.logical_and(k >= 1 + LAG2, k < NCH + 1 + LAG2))
        def _():
            second(k - 1 - LAG2)

        @pl.when(jnp.logical_and(k >= 1 + LAGF, k < NCH + 1 + LAGF))
        def _():
            final(k - 1 - LAGF)

        @pl.when(jnp.logical_and(k >= KEYS0, k < KEYS0 + NCH))
        def _():
            keys_step(k - KEYS0)

        return carry

    lax.fori_loop(0, NCH + 1 + LAGF, step, 0)

    for q in range(4):
        lanes = pl.ds(q * 128, 128)
        keys_ref[:, lanes] = (acc[:, lanes] * rcol[...]).astype(BF)

    def waits(k, carry):
        sent(k)
        return carry

    lax.fori_loop(0, NCH, waits, 0)
    for h in range(2):
        for n in range(5):
            for way in range(2):
                for kind in range(2):
                    ag(h, n, way, kind).wait_send()
    for m in range(16):
        share(m).wait_send()
    for j in range(4):
        for way in range(2):
            if j or way:
                to_z(j, way).wait_send()

    for i in range(1, 8):
        src = lax.rem(z + i, 8)
        send(zs.at[0], zr.at[src], s_z.at[0, 0], r_z.at[src], partner).wait_recv()
    total = zr[0].astype(F32)
    for i in range(1, 8):
        total = total + zr[i].astype(F32)
    fin[x] = total.astype(BF)

    outs = [send(fin.at[x], fin.at[x], s_f.at[i - 1], r_f.at[x], at(x + i, y, z, c)) for i in (1, 3, 2)]
    for cp in outs:
        cp.start()
    for i in range(1, 4):
        src = lax.rem(x + i, 4)
        send(fin.at[src], fin.at[src], s_f.at[0], r_f.at[src], xl).wait_recv()
    row = jnp.concatenate([gain[pl.ds(2 * s, 1), :], gain[pl.ds(2 * s + 1, 1), :]], axis=1)
    for q in range(4):
        grad_ref[:, pl.ds(q * 128, 128)] = jnp.transpose(fin[q].astype(F32) * row)
    for cp in outs:
        cp.wait_send()


def per_device(tokens, norm_gain, codes, zero_points, scales, key_grad):
    hbm = pl.BlockSpec(memory_space=pl.ANY)
    vmem = pl.BlockSpec(memory_space=pltpu.VMEM)
    sem = pltpu.SemaphoreType.DMA
    v = pltpu.VMEM
    return pl.pallas_call(
        kernel,
        out_shape=(jax.ShapeDtypeStruct((TOK, KV), BF), jax.ShapeDtypeStruct((BLK, KV), F32)),
        in_specs=[hbm] * 6,
        out_specs=(vmem, vmem),
        scratch_shapes=[
            v((TOK, D), BF), v((32, BLK, KV), BF), v((64, 128), F32), v((BLK, KV), jnp.int32), v((2, KV), jnp.int32),
            v((2, KV), F32), v((TOK, KV), BF), v((KV, TOK), F32), v((KV, TOK), BF), v((TOK, 128), F32),
            v((2, KV, BLK), F32), v((NCH, KV, BLK), BF), v((NCH, KV, BLK), BF), v((NCH, KV, BLK), BF),
            v((2, NCH, 64, BLK), BF), v((2, NCH, 64, BLK), BF), v((4, NCH, 64, BLK), BF),
            v((NCH, 128, BLK), BF), v((128, BLK), F32), v((12, 128, BLK), BF), v((4, 128, BLK), BF), v((8, 128, BLK), BF),
            v((4, 128, BLK), BF), v((TOK, KV), F32),
            sem((5 + NT,)), sem((NCH,)), sem((NCH,)), sem((2, NCH)), sem((2, NCH)), sem((4, NCH)), sem((4, NCH)),
            sem((12,)), sem((12,)), sem((4, 2)), sem((8,)), sem((3,)), sem((4,)), sem((40,)), sem((40,)), sem((16,)), sem((16,)),
        ],
        compiler_params=pltpu.CompilerParams(collective_id=1, has_side_effects=True, vmem_limit_bytes=56 * 2**20),
        cost_estimate=pl.CostEstimate(flops=8 * TOK * D * KV // 2, bytes_accessed=12 * 2**20, transcendentals=TOK),
        name="layer",
    )(tokens, norm_gain.reshape(64, 128), codes, zero_points, scales, key_grad)


def solution(mesh):
    in_specs = (
        P(("grp", "shard"), None),
        P(),
        P("shard", None),
        P("shard", None),
        P("shard", None),
        P(("grp", "shard"), None),
    )
    out_specs = (P(("grp", "shard"), None), P("shard", None))
    return jax.shard_map(
        per_device, mesh=mesh, in_specs=in_specs, out_specs=out_specs, check_vma=False
    )
```

time: 409 us -> 85 us (0.21); the launches traced: 403 us -> 84.8 us
  waiting for transfers between devices: 356 us -> 0 us
  Pallas kernels: 0 us -> 80.5 us
  matrix products: 24.4 us -> 0 us
  between operations: 13.8 us -> 0.64 us
  other arithmetic: 5.93 us -> 0 us
    reduce_scatter x1 -> x0, waiting for transfers between devices: 194 us -> none  [per_device(): lax.psum_scatter(lax.dot_general(columns, key_grad, (((0,), (0,)), ((), (...]
    psum x1 -> x0, waiting for transfers between devices: 93.3 us -> none  [per_device(): weight_grad = lax.psum(own_rows, 'grp')]
    pallas_call x0 -> x1, Pallas kernels: none -> 80.5 us  [per_device(): pl.pallas_call(kernel, out_shape=(jax.ShapeDtypeStruct((TOK, KV), BF), ja...]
    all_gather x1 -> x0, waiting for transfers between devices: 69.3 us -> none  [per_device(): lax.all_gather(weight, 'shard', axis=0, tiled=True)]
    dot_general x2 -> x0, matrix products: 24.4 us -> none  [the longest x1 13.3 us: per_device(): lax.dot_general(columns, key_grad, (((0,), (0,)), ((), ())), preferred_el...]
    reduce_sum x1 -> x0, other arithmetic: 5.15 us -> none  [normalize(): mean_sq = jnp.mean(values * values, axis=-1, keepdims=True)]
  transfers between devices with their start and end apart: 3 -> 0, of which waited for: 3 -> 0; matrix products, arithmetic and copies ran while one was open for 3% -> 0% of each run, Pallas kernels for 0% -> 0%
where the time goes in v1:
time: 85 us; the launch traced here: 84.8 us
  Pallas kernels  80.5 us (95%)
  local copies, waits for them, and re-layouts  3.74 us (4%)
    pallas_call x1, Pallas kernels, per_device(): pl.pallas_call(kernel, out_shape=(jax.ShapeDtypeStruct((TOK, KV), BF), ja...  80.5 us
    unnamed x2, local copies, waits for them, and re-layouts  3.74 us

profile of v1, /device:TPU:2, one launch (start us, length us, event | category | flops | bytes accessed | tf_op | source)
XLA Modules:
  0.0 84.8 jit_solution(14672418097890268677)
XLA Ops:
  0.6 80.5 %layer.1 = (bf16[512,512]{1,0:T(8,128)(2,1)}, f32[256,512]{1,0:T(8,128)}) custom-call(bf16[512,8192]{1,0:T(8,128)(2,1)} %tok_h.1, f32[64,128]{1,0:T(8,128)} %bitcast.1, s32[256,512]{1,0:T(8,128)} %codes_h.1, s32[2,512]{1,0:T(2,128)} %zp_h.1, f32[2,512]{1,0:T(2,128)} %sc_h.1, bf16[512,512]{1,0:T(8,128)(2,1)} %kg_h.1), custom_call_target="tpu_custom_call" | custom-call | flops 8589934592 | bytes 12582912 | tf_op jit(solution)/shard_map/layer/pallas_call | solution.py:364
  81.1 1.9 %copy.10 = bf16[512,512]{1,0:T(8,128)(2,1)} copy(bf16[512,512]{1,0:T(8,128)(2,1)} %get-tuple-element.4) | data formatting | bytes 1048576
  83.0 1.9 %copy.11 = f32[256,512]{1,0:T(8,128)} copy(f32[256,512]{1,0:T(8,128)} %get-tuple-element.5) | data formatting | bytes 1048576

commit v2 on v1

v2 whole, which is shorter than its diff:
```python
import jax
import jax.numpy as jnp
from jax import lax
from jax.experimental import pallas as pl
from jax.experimental.pallas import tpu as pltpu
from jax.sharding import PartitionSpec as P

EPS = 1e-05
D, KV, TOK = 8192, 512, 512
BLK = 256
MESH = pl.DeviceIdType.MESH
BF, F32 = jnp.bfloat16, jnp.float32
ORDER = (0, 1, 3, 2)
PIECES = ((2, 0), (3, 1), (2, 1), (1, 0), (3, 0), (1, 1), (0, 0), (0, 1))
BLOCKS = [(0, 0), (0, 1), (0, 3), (1, 0), (3, 0), (0, 2), (2, 0), (1, 1), (1, 3), (3, 1), (3, 3), (1, 2), (3, 2), (2, 1), (2, 3), (2, 2)]
NCH = 13
YPOS = 11
YSEC = 6
CUT = 192
LAG2 = 2
LAGF = 5
LAGS = 8
SLOT_A = 1
SLOT_B = 7
SLOT_C = 12
SLOT_B0 = 5
KEYS0 = 9
NT = 16
FLY = 6


def gray(i):
    return i + (i // 2) * (1 - 2 * (i % 2))


def pick(table, m):
    value = table[0]
    for n in range(1, len(table)):
        value = jnp.where(m == n, table[n], value)
    return value


def kernel(tok_h, gain_h, codes_h, zp_h, sc_h, kg_h, keys_h, fin_h,
           t, w, gain, codes, zp, sc, kg, kt, rkt, rcol, own, psend, prec, comb, xt, xs, xf, ys, ysum, yr, zs, zr, fin, acc, keys_ref,
           yc, yt, yd, yu, ye, s_yy, r_yy,
           lsem, s_l, r_l, s_p, r_p, s_xt, r_xt, s_xf, r_xf, s_y, r_y, s_z, r_z, s_f, r_f, s_ag, r_ag, s_w, r_w):
    g, s = lax.axis_index("grp"), lax.axis_index("shard")
    x, zh = lax.rem(g, 4), lax.div(g, 4)
    y, zl, c = lax.div(s, 8), lax.rem(lax.div(s, 2), 4), lax.rem(s, 2)
    z = zh * 4 + zl

    def at(ax, ay, az, ac):
        ax, ay, az = lax.rem(ax, 4), lax.rem(ay, 4), lax.rem(az, 8)
        return (lax.div(az, 4) * 4 + ax, (ay * 4 + lax.rem(az, 4)) * 2 + ac)

    partner = at(x, y, z, 1 - c)
    xl, xr = at(x + 3, y, z, c), at(x + 1, y, z, c)
    hop = {("y", 0): at(x, y + 1, z, c), ("y", 1): at(x, y + 3, z, c), ("z", 0): at(x, y, z + 1, c), ("z", 1): at(x, y, z + 7, c)}

    def block(dy, dz, core):
        return (lax.rem(y + dy, 4) * 4 + lax.rem(zl + dz, 4)) * 2 + core

    def send(src, dst, ss, rs, to):
        return pltpu.make_async_remote_copy(src_ref=src, dst_ref=dst, send_sem=ss, recv_sem=rs, device_id=to, device_id_type=MESH)

    barrier = pltpu.get_barrier_semaphore()
    peers = [partner] + [at(x + i, y, z, c) for i in (1, 2, 3)] + [at(x, y + i, z, c) for i in (1, 2, 3)]
    peers += [at(x, y, z + i, c) for i in range(1, 8)]
    for p in peers:
        pl.semaphore_signal(barrier, inc=1, device_id=p, device_id_type=MESH)

    loads = [pltpu.make_async_copy(a, b, lsem.at[i]) for i, (a, b) in enumerate(
        [(codes_h, codes), (zp_h, zp), (sc_h, sc), (gain_h, gain), (kg_h, kg)])]
    for cp in loads:
        cp.start()
    rows_t = TOK // NT

    def load_t(i):
        r = pl.ds(pl.multiple_of(i * rows_t, rows_t), rows_t)
        return pltpu.make_async_copy(tok_h.at[r], t.at[r], lsem.at[5 + i])

    for i in range(FLY):
        load_t(i).start()

    for cp in loads[:4]:
        cp.wait()
    mine = block(0, 0, c)
    for j in range(2):
        row = gain[pl.ds(2 * s + j, 1), :]
        col = jnp.transpose(jnp.broadcast_to(row, (128, 128)))
        part = pl.ds(j * 128, 128)
        for q in range(4):
            lanes = pl.ds(q * 128, 128)
            shaped = (codes[part, lanes] - zp[pl.ds(j, 1), lanes]).astype(F32)
            w[mine, part, lanes] = (shaped * sc[pl.ds(j, 1), lanes] * col).astype(BF)

    pl.semaphore_wait(barrier, len(peers))

    def ag(h, n, way, kind):
        axis = ("y", "z")[(h + (n > 0)) % 2]
        dp = ORDER[n - 1] if n > 0 else 0
        off = 0 if kind == 0 else (3, 1)[way]
        if n == 0:
            dp, dq = off, 0
        else:
            dq = off
        dy, dz = (dp, dq) if h == 0 else (dq, dp)
        size = (CUT, BLK - CUT)[h]
        lo = h * CUT
        if kind == 1:
            size = size // 2
            lo = lo + size * way
        ref = w.at[block(dy, dz, c), pl.ds(lo, size)]
        i = ((h * 5 + n) * 2 + way) * 2 + kind
        return send(ref, ref, s_ag.at[i], r_ag.at[i], hop[(axis, way)])

    def ag_start(n, kind):
        for h in range(2):
            for way in range(2):
                ag(h, n, way, kind).start()

    def ag_wait(n, kind):
        for h in range(2):
            for way in range(2):
                ag(h, n, way, kind).wait_recv()

    def share(m):
        dy, dz = BLOCKS[m]
        ref = w.at[block(dy, dz, c)]
        return send(ref, ref, s_w.at[m], r_w.at[m], partner)

    ag_start(0, 0)
    ag_start(1, 0)
    share(0).start()

    loads[4].wait()
    kt[...] = jnp.transpose(kg[...].astype(F32))

    def norm_rows(i, carry):
        load_t(i).wait()

        @pl.when(i + FLY < NT)
        def _():
            load_t(i + FLY).start()

        def tile(u, carry):
            r0 = pl.multiple_of(i * rows_t + u * 16, 16)
            sums = [jnp.zeros((16, 128), F32) for _ in range(4)]
            for v in range(D // 128):
                val = t[pl.ds(r0, 16), pl.ds(v * 128, 128)].astype(F32)
                sums[v % 4] = sums[v % 4] + val * val
            total = jnp.sum((sums[0] + sums[1]) + (sums[2] + sums[3]), axis=1, keepdims=True)
            rcol[pl.ds(r0, 16), :] = jnp.broadcast_to(lax.rsqrt(total * (1.0 / D) + EPS), (16, 128))
            return carry

        return lax.fori_loop(0, rows_t // 16, tile, carry)

    lax.fori_loop(0, NT, norm_rows, 0)
    for q in range(4):
        lanes = pl.ds(q * 128, 128)
        row = jnp.transpose(rcol[lanes, :])[0:1, :]
        for i, (dx, half) in enumerate(PIECES):
            src = pl.ds(pl.multiple_of(lax.rem(x + dx, 4) * 128 + half * 64, 64), 64)
            rkt[pl.ds(i * 64, 64), lanes] = (kt[src, lanes] * row).astype(BF)

    def place(k):
        e = k - (k > YPOS).astype(jnp.int32)
        return e // 4, e % 4

    def term(b):
        cols = pl.ds(pl.multiple_of(b * BLK, BLK), BLK)
        return jnp.dot(rkt[...], t[:, cols], preferred_element_type=F32)

    def to_partner(n):
        return send(psend.at[n], prec.at[n], s_p.at[n], r_p.at[n], partner)

    def part(i):
        return pl.ds(64 * i, 64)

    def x_first(k):
        return [
            send(comb.at[k, pl.ds(0, 128)], xt.at[1, k], s_xt.at[1, k], r_xt.at[1, k], xl),
            send(comb.at[k, pl.ds(128, 128)], xt.at[0, k], s_xt.at[0, k], r_xt.at[0, k], xr),
        ]

    def x_second(k):
        return [
            send(xs.at[0, k], xf.at[0, k], s_xf.at[0, k], r_xf.at[0, k], xl),
            send(xs.at[1, k], xf.at[1, k], s_xf.at[1, k], r_xf.at[1, k], xr),
        ]

    def to_y(jj, i):
        n = jj * 3 + i
        return send(ys.at[n], yr.at[n], s_y.at[n], r_y.at[n], at(x, y + gray(3 - i), z, c))

    def to_z(j, way):
        to = at(x, y, z + gray(j) + 4 * way, c)
        return send(zs.at[j], zr.at[z], s_z.at[j, way], r_z.at[z], to)

    def last_z(way, half):
        rows = part(half)
        return send(zs.at[3, rows], zr.at[z, rows], s_l.at[way, half], r_l.at[way, half], at(x, y, z + 2 + 4 * way, c))

    def to_x(i, half):
        rows = part(half)
        return send(fin.at[rows], fin_h.at[x, rows], s_f.at[i - 1, half], r_f.at[x, half], at(x + i, y, z, c))

    def gradient(n, dy, dz, held):
        psend[n] = term(block(dy, dz, 1 - c)).astype(BF)
        to_partner(n).start()
        own[held] = term(block(dy, dz, c))

    def both(n, held):
        to_partner(n).wait_recv()
        return (own[held] + prec[n].astype(F32)).astype(BF)

    upper, lower = pl.ds(0, 256), pl.ds(256, 256)

    def y_pass(i):
        src, dst, way = (
            (yc.at[0, upper], yt.at[0], 1),
            (yc.at[0, lower], yt.at[1], 0),
            (yc.at[2, upper], yd.at[0], 0),
            (yc.at[1, lower], yd.at[1], 1),
            (yu.at[0], ye.at[0], 1),
            (yu.at[1], ye.at[1], 0),
        )[i]
        return send(src, dst, s_yy.at[i], r_yy.at[i], hop[("y", way)])

    def y_second():
        y_pass(0).wait_recv()
        yu[0] = (yc[1, upper, :].astype(F32) + yt[0].astype(F32)).astype(BF)
        y_pass(4).start()
        y_pass(1).wait_recv()
        yu[1] = (yc[2, lower, :].astype(F32) + yt[1].astype(F32)).astype(BF)
        y_pass(5).start()

    def y_final():
        for i in (2, 4):
            y_pass(i).wait_recv()
        comb[YPOS, upper, :] = (yc[3, upper, :].astype(F32) + yd[0].astype(F32) + ye[0].astype(F32)).astype(BF)
        for i in (3, 5):
            y_pass(i).wait_recv()
        comb[YPOS, lower, :] = (yc[3, lower, :].astype(F32) + yd[1].astype(F32) + ye[1].astype(F32)).astype(BF)

    def second(k):
        first = x_first(k)
        later = x_second(k)
        for i in range(2):
            first[i].wait_recv()
            xs[i, k] = (comb[k, part(4 + i), :].astype(F32) + xt[1 - i, k, part(0), :].astype(F32)).astype(BF)
            later[i].start()

    def x_sum(k, half):
        x_second(k)[half].wait_recv()
        return comb[k, part(6 + half), :].astype(F32) + xt[half, k, part(1), :].astype(F32) + xf[half, k].astype(F32)

    def y_sum(jj, half, total):
        for i in range(3):
            total = total + yr[jj * 3 + i, part(half), :].astype(F32)
        return total.astype(BF)

    def final(k):
        jj, i = place(k)

        @pl.when(k == YPOS)
        def _():
            for half in range(2):
                zs[0, part(half), :] = x_sum(k, half).astype(BF)
            zr[z] = zs[0]
            to_z(0, 1).start()

        @pl.when(jnp.logical_and(k != YPOS, i != 3))
        def _():
            for half in range(2):
                ys[jj * 3 + i, part(half), :] = x_sum(k, half).astype(BF)
            to_y(jj, i).start()

        @pl.when(jnp.logical_and(k != YPOS, i == 3))
        def _():
            for n in range(3):
                to_y(jj, n).wait_recv()
            for half in range(2):
                zs[jj + 1, part(half), :] = y_sum(jj, half, x_sum(k, half))
            to_z(jj + 1, 0).start()
            to_z(jj + 1, 1).start()

    def last():
        k = NCH - 1
        for half in range(2):
            total = x_sum(k, half)
            if half == 0:
                for i in range(3):
                    to_y(2, i).wait_recv()
            zs[3, part(half), :] = y_sum(2, half, total)
            for way in range(2):
                last_z(way, half).start()

    def sent(k):
        jj, i = place(k)
        for cp in x_first(k) + x_second(k):
            cp.wait_send()

        @pl.when(k != YPOS)
        def _():
            to_partner(k).wait_send()

        @pl.when(jnp.logical_and(k != YPOS, i != 3))
        def _():
            to_y(jj, i).wait_send()

    def keys_step(m):
        dy, dz = pick([b[0] for b in BLOCKS], m), pick([b[1] for b in BLOCKS], m)
        ref = w.at[block(dy, dz, 1 - c)]
        send(ref, ref, s_w.at[m], r_w.at[m], partner).wait_recv()
        for core in range(2):
            b = block(dy, dz, core)
            cols = pl.ds(pl.multiple_of(b * BLK, BLK), BLK)
            acc[...] += jnp.dot(t[:, cols], w[b], preferred_element_type=F32)

    acc[...] = jnp.zeros_like(acc)

    def step(k, carry):
        @pl.when(jnp.logical_and(k < NCH, k != YPOS))
        def _():
            jj, i = place(k)
            gradient(k, gray(3 - i), gray(jj + 1), k % 2)

        @pl.when(jnp.logical_and(k >= 1, k < NCH + 1))
        def _():
            @pl.when(k - 1 != YPOS)
            def _():
                comb[k - 1] = both(k - 1, (k - 1) % 2)

            @pl.when(k - 1 == YPOS)
            def _():
                y_final()

            for cp in x_first(k - 1):
                cp.start()

        @pl.when(k < 4)
        def _():
            gradient(NCH + k, gray(3 - k), 0, 2 + k % 2)

        @pl.when(jnp.logical_and(k >= 1, k < 5))
        def _():
            yc[k - 1] = both(NCH + k - 1, 2 + (k - 1) % 2)

        @pl.when(k == 1)
        def _():
            y_pass(0).start()
            y_pass(1).start()

        @pl.when(k == 2)
        def _():
            y_pass(3).start()

        @pl.when(k == 3)
        def _():
            y_pass(2).start()

        @pl.when(k == YSEC)
        def _():
            y_second()

        @pl.when(k == SLOT_A)
        def _():
            ag_wait(0, 0)
            ag_start(0, 1)
            ag_start(2, 0)
            ag_start(3, 0)
            ag_wait(1, 0)
            ag_start(1, 1)
            for m in range(1, 5):
                share(m).start()

        @pl.when(k == SLOT_B0)
        def _():
            ag_wait(0, 1)
            ag_start(4, 0)
            ag_wait(2, 0)
            ag_start(2, 1)

        @pl.when(k == SLOT_B)
        def _():
            ag_wait(3, 0)
            ag_start(3, 1)
            ag_wait(1, 1)
            for m in range(5, 11):
                share(m).start()

        @pl.when(k == SLOT_C)
        def _():
            ag_wait(4, 0)
            ag_start(4, 1)
            ag_wait(2, 1)
            ag_wait(3, 1)
            for m in range(11, 15):
                share(m).start()

        @pl.when(jnp.logical_and(k >= 1 + LAG2, k < NCH + 1 + LAG2))
        def _():
            second(k - 1 - LAG2)

        @pl.when(jnp.logical_and(k >= 1 + LAGF, k < NCH + LAGF))
        def _():
            final(k - 1 - LAGF)

        @pl.when(k >= KEYS0)
        def _():
            keys_step(k - KEYS0)

        @pl.when(k >= LAGS)
        def _():
            sent(k - LAGS)

        return carry

    lax.fori_loop(0, NCH + LAGF, step, 0)
    last()
    ag_wait(4, 1)
    share(15).start()

    def keys_rest(m, carry):
        keys_step(m)
        return carry

    lax.fori_loop(NCH + LAGF - KEYS0, len(BLOCKS), keys_rest, 0)


    for q in range(4):
        lanes = pl.ds(q * 128, 128)
        keys_ref[:, lanes] = (acc[:, lanes] * rcol[...]).astype(BF)
    out_keys = pltpu.make_async_copy(keys_ref, keys_h, lsem.at[0])
    out_keys.start()

    def slot(i):
        return lax.rem(z + i, 8)

    for i in (1, 3, 4, 5, 7):
        send(zs.at[0], zr.at[slot(i)], s_z.at[0, 0], r_z.at[slot(i)], partner).wait_recv()

    def pair(i, rows):
        return zr[slot(i), rows, :].astype(F32) + zr[slot(i + 4), rows, :].astype(F32)

    everything = pl.ds(0, 128)
    ysum[...] = pair(0, everything) + pair(1, everything) + pair(3, everything)

    for half in range(2):
        rows = pl.ds(64 * half, 64)
        for way in range(2):
            last_z(way, half).wait_recv()
        fin[rows, :] = (ysum[rows, :] + pair(2, rows)).astype(BF)
        for i in (2, 1, 3):
            to_x(i, half).start()
    out_fin = pltpu.make_async_copy(fin, fin_h.at[x], lsem.at[1])
    out_fin.start()

    def waits(k, carry):
        sent(k)
        return carry

    lax.fori_loop(NCH + LAGF - LAGS, NCH, waits, 0)
    for i in range(6):
        y_pass(i).wait_send()
    for n in range(4):
        to_partner(NCH + n).wait_send()
    for h in range(2):
        for n in range(5):
            for way in range(2):
                for kind in range(2):
                    ag(h, n, way, kind).wait_send()
    for m in range(16):
        share(m).wait_send()
    for j in range(3):
        for way in range(2):
            if j or way:
                to_z(j, way).wait_send()
    for way in range(2):
        for half in range(2):
            last_z(way, half).wait_send()
    for i in range(1, 4):
        for half in range(2):
            to_x(i, half).wait_send()
    out_keys.wait()
    out_fin.wait()
    for i in range(1, 4):
        for half in range(2):
            src = lax.rem(x + i, 4)
            rows = pl.ds(64 * half, 64)
            send(fin.at[rows], fin_h.at[src, rows], s_f.at[0, half], r_f.at[src, half], xl).wait_recv()


def finish(keys_in, fin_in, gain_in, keys_out, grad_out, keys, fin, gain, grad, sems):
    s = lax.axis_index("shard")
    ins = [pltpu.make_async_copy(a, b, sems.at[i]) for i, (a, b) in enumerate([(keys_in, keys), (fin_in, fin), (gain_in, gain)])]
    for cp in ins:
        cp.start()
    ins[0].wait()
    out_keys = pltpu.make_async_copy(keys, keys_out, sems.at[3])
    out_keys.start()
    ins[1].wait()
    ins[2].wait()
    row = jnp.concatenate([gain[pl.ds(2 * s, 1), :], gain[pl.ds(2 * s + 1, 1), :]], axis=1)
    for q in range(4):
        grad[:, pl.ds(q * 128, 128)] = jnp.transpose(fin[q].astype(F32) * row)
    out_grad = pltpu.make_async_copy(grad, grad_out, sems.at[4])
    out_grad.start()
    out_keys.wait()
    out_grad.wait()


def per_device(tokens, norm_gain, codes, zero_points, scales, key_grad):
    hbm = pl.BlockSpec(memory_space=pl.ANY)
    sem = pltpu.SemaphoreType.DMA
    v = pltpu.VMEM
    norm_gain = norm_gain.reshape(64, 128)
    keys, summed = pl.pallas_call(
        kernel,
        out_shape=(jax.ShapeDtypeStruct((TOK, KV), BF), jax.ShapeDtypeStruct((4, 128, BLK), BF)),
        in_specs=[hbm] * 6,
        out_specs=(hbm, hbm),
        scratch_shapes=[
            v((TOK, D), BF), v((32, BLK, KV), BF), v((64, 128), F32), v((BLK, KV), jnp.int32), v((2, KV), jnp.int32),
            v((2, KV), F32), v((TOK, KV), BF), v((KV, TOK), F32), v((KV, TOK), BF), v((TOK, 128), F32),
            v((4, KV, BLK), F32), v((NCH + 4, KV, BLK), BF), v((NCH + 4, KV, BLK), BF), v((NCH, KV, BLK), BF),
            v((2, NCH, 128, BLK), BF), v((2, NCH, 64, BLK), BF), v((2, NCH, 64, BLK), BF),
            v((9, 128, BLK), BF), v((128, BLK), F32), v((9, 128, BLK), BF), v((4, 128, BLK), BF), v((8, 128, BLK), BF),
            v((128, BLK), BF), v((TOK, KV), F32), v((TOK, KV), BF),
            v((4, KV, BLK), BF), v((2, 256, BLK), BF), v((2, 256, BLK), BF), v((2, 256, BLK), BF), v((2, 256, BLK), BF), sem((6,)), sem((6,)),
            sem((5 + NT,)), sem((2, 2)), sem((2, 2)), sem((NCH + 4,)), sem((NCH + 4,)), sem((2, NCH)), sem((2, NCH)), sem((2, NCH)), sem((2, NCH)),
            sem((9,)), sem((9,)), sem((4, 2)), sem((8,)), sem((3, 2)), sem((4, 2)), sem((40,)), sem((40,)), sem((16,)), sem((16,)),
        ],
        compiler_params=pltpu.CompilerParams(collective_id=1, has_side_effects=True, vmem_limit_bytes=56 * 2**20),
        cost_estimate=pl.CostEstimate(flops=8 * TOK * D * KV // 2, bytes_accessed=12 * 2**20, transcendentals=TOK),
        name="layer",
    )(tokens, norm_gain, codes, zero_points, scales, key_grad)
    return pl.pallas_call(
        finish,
        out_shape=(jax.ShapeDtypeStruct((TOK, KV), BF), jax.ShapeDtypeStruct((BLK, KV), F32)),
        in_specs=[hbm] * 3,
        out_specs=(hbm, hbm),
        scratch_shapes=[v((TOK, KV), BF), v((4, 128, BLK), BF), v((64, 128), F32), v((BLK, KV), F32), sem((5,))],
        name="finish",
    )(keys, summed, norm_gain)


def solution(mesh):
    in_specs = (
        P(("grp", "shard"), None),
        P(),
        P("shard", None),
        P("shard", None),
        P("shard", None),
        P(("grp", "shard"), None),
    )
    out_specs = (P(("grp", "shard"), None), P("shard", None))
    return jax.shard_map(
        per_device, mesh=mesh, in_specs=in_specs, out_specs=out_specs, check_vma=False
    )
```

time: 85 us -> 70.5 us (0.83)
  Pallas kernels: 80.5 us -> 69.8 us
  local copies, waits for them, and re-layouts: 3.74 us -> 0 us
    pallas_call x1, Pallas kernels: 80.5 us -> 67.6 us  [per_device(): pl.pallas_call(kernel, out_shape=(jax.ShapeDtypeStruct((TOK, KV), BF), ja...]
    unnamed x2 -> x0, local copies, waits for them, and re-layouts: 3.74 us -> none
    pallas_call x0 -> x1, Pallas kernels: none -> 2.15 us  [per_device(): pl.pallas_call(finish, out_shape=(jax.ShapeDtypeStruct((TOK, KV), BF), ja...]
where the time goes in v2:
time: 70.5 us; the launch traced here: 70.4 us
  Pallas kernels  69.8 us (99%)
    pallas_call x1, Pallas kernels, per_device(): pl.pallas_call(kernel, out_shape=(jax.ShapeDtypeStruct((TOK, KV), BF), ja...  67.6 us
    pallas_call x1, Pallas kernels, per_device(): pl.pallas_call(finish, out_shape=(jax.ShapeDtypeStruct((TOK, KV), BF), ja...  2.15 us

profile of v2, /device:TPU:2, one launch (start us, length us, event | category | flops | bytes accessed | tf_op | source)
XLA Modules:
  0.0 70.4 jit_solution(772669259410267407)
XLA Ops:
  0.6 67.6 %layer.1 = (bf16[512,512]{1,0:T(8,128)(2,1)}, bf16[4,128,256]{2,1,0:T(8,128)(2,1)}) custom-call(bf16[512,8192]{1,0:T(8,128)(2,1)} %tok_h.1, f32[64,128]{1,0:T(8,128)} %bitcast.1, s32[256,512]{1,0:T(8,128)} %codes_h.1, s32[2,512]{1,0:T(2,128)} %zp_h.1, f32[2,512]{1,0:T(2,128)} %sc_h.1, bf16[512,512]{1,0:T(8,128)(2,1)} %kg_h.1), custom_call_target="tpu_custom_call" | custom-call | flops 8589934592 | bytes 12582912 | tf_op jit(solution)/shard_map/layer/pallas_call | solution.py:519
  68.3 2.1 %finish.1 = (bf16[512,512]{1,0:T(8,128)(2,1)}, f32[256,512]{1,0:T(8,128)}) custom-call(bf16[512,512]{1,0:T(8,128)(2,1)} %get-tuple-element.4.keys_in, bf16[4,128,256]{2,1,0:T(8,128)(2,1)} %get-tuple-element.5.fin_in, f32[64,128]{1,0:T(8,128)} %bitcast.2), custom_call_target="tpu_custom_call" | custom-call | tf_op jit(solution)/shard_map/finish/pallas_call | solution.py:539

commit v3 on v2

--- a/solution.py
+++ b/solution.py
@@ -14,9 +14,10 @@
 PIECES = ((2, 0), (3, 1), (2, 1), (1, 0), (3, 0), (1, 1), (0, 0), (0, 1))
 BLOCKS = [(0, 0), (0, 1), (0, 3), (1, 0), (3, 0), (0, 2), (2, 0), (1, 1), (1, 3), (3, 1), (3, 3), (1, 2), (3, 2), (2, 1), (2, 3), (2, 2)]
 NCH = 13
-YPOS = 11
-YSEC = 6
-CUT = 192
+YPOS = 10
+YSEC = 7
+Y0 = 2
+CUT = 224
 LAG2 = 2
 LAGF = 5
 LAGS = 8
@@ -24,7 +25,7 @@
 SLOT_B = 7
 SLOT_C = 12
 SLOT_B0 = 5
-KEYS0 = 9
+KEYS0 = 8
 NT = 16
 FLY = 6
 
@@ -63,24 +64,24 @@
     def send(src, dst, ss, rs, to):
         return pltpu.make_async_remote_copy(src_ref=src, dst_ref=dst, send_sem=ss, recv_sem=rs, device_id=to, device_id_type=MESH)
 
+    loads = [pltpu.make_async_copy(a, b, lsem.at[i]) for i, (a, b) in enumerate(
+        [(codes_h, codes), (zp_h, zp), (sc_h, sc), (gain_h, gain), (kg_h, kg)])]
+    for cp in loads:
+        cp.start()
+    rows_t = TOK // NT
+
+    def load_t(i):
+        r = pl.ds(pl.multiple_of(i * rows_t, rows_t), rows_t)
+        return pltpu.make_async_copy(tok_h.at[r], t.at[r], lsem.at[5 + i])
+
+    for i in range(FLY):
+        load_t(i).start()
+
     barrier = pltpu.get_barrier_semaphore()
     peers = [partner] + [at(x + i, y, z, c) for i in (1, 2, 3)] + [at(x, y + i, z, c) for i in (1, 2, 3)]
     peers += [at(x, y, z + i, c) for i in range(1, 8)]
     for p in peers:
         pl.semaphore_signal(barrier, inc=1, device_id=p, device_id_type=MESH)
-
-    loads = [pltpu.make_async_copy(a, b, lsem.at[i]) for i, (a, b) in enumerate(
-        [(codes_h, codes), (zp_h, zp), (sc_h, sc), (gain_h, gain), (kg_h, kg)])]
-    for cp in loads:
-        cp.start()
-    rows_t = TOK // NT
-
-    def load_t(i):
-        r = pl.ds(pl.multiple_of(i * rows_t, rows_t), rows_t)
-        return pltpu.make_async_copy(tok_h.at[r], t.at[r], lsem.at[5 + i])
-
-    for i in range(FLY):
-        load_t(i).start()
 
     for cp in loads[:4]:
         cp.wait()
@@ -313,10 +314,9 @@
         dy, dz = pick([b[0] for b in BLOCKS], m), pick([b[1] for b in BLOCKS], m)
         ref = w.at[block(dy, dz, 1 - c)]
         send(ref, ref, s_w.at[m], r_w.at[m], partner).wait_recv()
-        for core in range(2):
-            b = block(dy, dz, core)
-            cols = pl.ds(pl.multiple_of(b * BLK, BLK), BLK)
-            acc[...] += jnp.dot(t[:, cols], w[b], preferred_element_type=F32)
+        b = block(dy, dz, 0)
+        cols = pl.ds(pl.multiple_of(b * BLK, 2 * BLK), 2 * BLK)
+        acc[...] += jnp.dot(t[:, cols], w[pl.ds(b, 2)].reshape(2 * BLK, KV), preferred_element_type=F32)
 
     acc[...] = jnp.zeros_like(acc)
 
@@ -339,24 +339,26 @@
             for cp in x_first(k - 1):
                 cp.start()
 
-        @pl.when(k < 4)
-        def _():
-            gradient(NCH + k, gray(3 - k), 0, 2 + k % 2)
-
-        @pl.when(jnp.logical_and(k >= 1, k < 5))
-        def _():
-            yc[k - 1] = both(NCH + k - 1, 2 + (k - 1) % 2)
-
-        @pl.when(k == 1)
+        @pl.when(jnp.logical_and(k >= Y0, k < Y0 + 4))
+        def _():
+            i = k - Y0
+            gradient(NCH + i, gray(3 - i), 0, 2 + i % 2)
+
+        @pl.when(jnp.logical_and(k >= Y0 + 1, k < Y0 + 5))
+        def _():
+            i = k - Y0 - 1
+            yc[i] = both(NCH + i, 2 + i % 2)
+
+        @pl.when(k == Y0 + 1)
         def _():
             y_pass(0).start()
             y_pass(1).start()
 
-        @pl.when(k == 2)
+        @pl.when(k == Y0 + 2)
         def _():
             y_pass(3).start()
 
-        @pl.when(k == 3)
+        @pl.when(k == Y0 + 3)
         def _():
             y_pass(2).start()
 
@@ -494,21 +496,24 @@
 
 def finish(keys_in, fin_in, gain_in, keys_out, grad_out, keys, fin, gain, grad, sems):
     s = lax.axis_index("shard")
-    ins = [pltpu.make_async_copy(a, b, sems.at[i]) for i, (a, b) in enumerate([(keys_in, keys), (fin_in, fin), (gain_in, gain)])]
+    ins = [pltpu.make_async_copy(a, b, sems.at[i]) for i, (a, b) in enumerate([(fin_in, fin), (gain_in, gain), (keys_in, keys)])]
     for cp in ins:
         cp.start()
     ins[0].wait()
-    out_keys = pltpu.make_async_copy(keys, keys_out, sems.at[3])
-    out_keys.start()
     ins[1].wait()
-    ins[2].wait()
     row = jnp.concatenate([gain[pl.ds(2 * s, 1), :], gain[pl.ds(2 * s + 1, 1), :]], axis=1)
+    outs = []
     for q in range(4):
-        grad[:, pl.ds(q * 128, 128)] = jnp.transpose(fin[q].astype(F32) * row)
-    out_grad = pltpu.make_async_copy(grad, grad_out, sems.at[4])
-    out_grad.start()
-    out_keys.wait()
-    out_grad.wait()
+        lanes = pl.ds(q * 128, 128)
+        grad[:, lanes] = jnp.transpose(fin[q].astype(F32) * row)
+        outs.append(pltpu.make_async_copy(grad.at[:, lanes], grad_out.at[:, lanes], sems.at[3 + q]))
+        outs[-1].start()
+        if q == 1:
+            ins[2].wait()
+            outs.append(pltpu.make_async_copy(keys, keys_out, sems.at[7]))
+            outs[-1].start()
+    for cp in outs:
+        cp.wait()
 
 
 def per_device(tokens, norm_gain, codes, zero_points, scales, key_grad):
@@ -541,7 +546,7 @@
         out_shape=(jax.ShapeDtypeStruct((TOK, KV), BF), jax.ShapeDtypeStruct((BLK, KV), F32)),
         in_specs=[hbm] * 3,
         out_specs=(hbm, hbm),
-        scratch_shapes=[v((TOK, KV), BF), v((4, 128, BLK), BF), v((64, 128), F32), v((BLK, KV), F32), sem((5,))],
+        scratch_shapes=[v((TOK, KV), BF), v((4, 128, BLK), BF), v((64, 128), F32), v((BLK, KV), F32), sem((8,))],
         name="finish",
     )(keys, summed, norm_gain)
 

time: 70.5 us -> 67.8 us (0.962)
  Pallas kernels: 69.8 us -> 67 us
    pallas_call x1, Pallas kernels: 67.6 us -> 64.9 us  [per_device(): pl.pallas_call(kernel, out_shape=(jax.ShapeDtypeStruct((TOK, KV), BF), ja...]
where the time goes in v3:
time: 67.8 us; the launch traced here: 67.7 us
  Pallas kernels  67 us (99%)
    pallas_call x1, Pallas kernels, per_device(): pl.pallas_call(kernel, out_shape=(jax.ShapeDtypeStruct((TOK, KV), BF), ja...  64.9 us
    pallas_call x1, Pallas kernels, per_device(): pl.pallas_call(finish, out_shape=(jax.ShapeDtypeStruct((TOK, KV), BF), ja...  2.09 us

profile of v3, /device:TPU:2, one launch (start us, length us, event | category | flops | bytes accessed | tf_op | source)
XLA Modules:
  0.0 67.7 jit_solution(16761887802193372128)
XLA Ops:
  0.6 64.9 %layer.1 = (bf16[512,512]{1,0:T(8,128)(2,1)}, bf16[4,128,256]{2,1,0:T(8,128)(2,1)}) custom-call(bf16[512,8192]{1,0:T(8,128)(2,1)} %tok_h.1, f32[64,128]{1,0:T(8,128)} %bitcast.1, s32[256,512]{1,0:T(8,128)} %codes_h.1, s32[2,512]{1,0:T(2,128)} %zp_h.1, f32[2,512]{1,0:T(2,128)} %sc_h.1, bf16[512,512]{1,0:T(8,128)(2,1)} %kg_h.1), custom_call_target="tpu_custom_call" | custom-call | flops 8589934592 | bytes 12582912 | tf_op jit(solution)/shard_map/layer/pallas_call | solution.py:524
  65.6 2.1 %finish.1 = (bf16[512,512]{1,0:T(8,128)(2,1)}, f32[256,512]{1,0:T(8,128)}) custom-call(bf16[512,512]{1,0:T(8,128)(2,1)} %get-tuple-element.4.keys_in, bf16[4,128,256]{2,1,0:T(8,128)(2,1)} %get-tuple-element.5.fin_in, f32[64,128]{1,0:T(8,128)} %bitcast.2), custom_call_target="tpu_custom_call" | custom-call | tf_op jit(solution)/shard_map/finish/pallas_call | solution.py:544

commit v4 on v3

--- a/solution.py
+++ b/solution.py
@@ -24,10 +24,10 @@
 SLOT_A = 1
 SLOT_B = 7
 SLOT_C = 12
-SLOT_B0 = 5
+SLOT_B0 = 4
 KEYS0 = 8
 NT = 16
-FLY = 6
+FLY = 8
 
 
 def gray(i):

time: 67.8 us -> 67.9 us (level)
  no operation moved by 1% of the time
where the time goes in v4:
time: 67.9 us; the launch traced here: 67.8 us
  Pallas kernels  67.2 us (99%)
    pallas_call x1, Pallas kernels, per_device(): pl.pallas_call(kernel, out_shape=(jax.ShapeDtypeStruct((TOK, KV), BF), ja...  65.1 us
    pallas_call x1, Pallas kernels, per_device(): pl.pallas_call(finish, out_shape=(jax.ShapeDtypeStruct((TOK, KV), BF), ja...  2.09 us

profile of v4, /device:TPU:2, one launch (start us, length us, event | category | flops | bytes accessed | tf_op | source)
XLA Modules:
  0.0 67.8 jit_solution(11803065458193717063)
XLA Ops:
  0.6 65.1 %layer.1 = (bf16[512,512]{1,0:T(8,128)(2,1)}, bf16[4,128,256]{2,1,0:T(8,128)(2,1)}) custom-call(bf16[512,8192]{1,0:T(8,128)(2,1)} %tok_h.1, f32[64,128]{1,0:T(8,128)} %bitcast.1, s32[256,512]{1,0:T(8,128)} %codes_h.1, s32[2,512]{1,0:T(2,128)} %zp_h.1, f32[2,512]{1,0:T(2,128)} %sc_h.1, bf16[512,512]{1,0:T(8,128)(2,1)} %kg_h.1), custom_call_target="tpu_custom_call" | custom-call | flops 8589934592 | bytes 12582912 | tf_op jit(solution)/shard_map/layer/pallas_call | solution.py:524
  65.8 2.1 %finish.1 = (bf16[512,512]{1,0:T(8,128)(2,1)}, f32[256,512]{1,0:T(8,128)}) custom-call(bf16[512,512]{1,0:T(8,128)(2,1)} %get-tuple-element.4.keys_in, bf16[4,128,256]{2,1,0:T(8,128)(2,1)} %get-tuple-element.5.fin_in, f32[64,128]{1,0:T(8,128)} %bitcast.2), custom_call_target="tpu_custom_call" | custom-call | tf_op jit(solution)/shard_map/finish/pallas_call | solution.py:544
